TPU v7x, 256 devices: a whole 4x4x8 slice. The times are simulated.
256 devices in a mesh: blk: 16 (over y, x_hi, core), bulk: 16 (over z, x_lo).
Axes of the slice: x: 4 (x_hi: 2, x_lo: 2; x = x_hi * 2 + x_lo), y: 4, z: 8, core: 2. Of those that a mesh axis runs over, the one named last changes fastest.
Arguments:
- amplitudes: bfloat16 [1600, 28800], P('blk', 'bulk'), may hold values from -6 to 6
- integrals: bfloat16 [28800, 28800], P('bulk', 'blk'), may hold values from -0.03125 to 0.03125
- cd_blocks: int32 [32, 2], P('bulk'), may hold values from 0 to 29, as said below
Outputs:
- ladder: float32 [1600, 28800], P('bulk', 'blk')
Inputs may be any that keep to these rules, and one draw needn't show every extreme that they name: `cd_blocks`: each row holds two virtual block numbers below 30, the first not greater than the second.
All inputs are finite; a program needn't handle non-finite values.
Results may differ from a plain program's by a relative error of at most 0.0003.
Values may be sent and summed in bfloat16 or wider, within the bound.
A program may use at most 128 MiB of HBM per device.

v0:
```python
import jax
import jax.numpy as jnp
from jax import lax
from jax.sharding import PartitionSpec as P


def on_device(amplitudes, integrals, cd_blocks):
    per_block = integrals.shape[0] // cd_blocks.shape[0]
    factor = 2.0 - (cd_blocks[:, 0] == cd_blocks[:, 1]).astype(jnp.float32)
    pair_weight = jnp.repeat(factor, per_block)
    panel = (integrals.astype(jnp.float32) * pair_weight[:, None]).astype(jnp.bfloat16)
    partial_value = jnp.dot(
        lax.all_gather(amplitudes, "blk", axis=0, tiled=True),
        panel,
        preferred_element_type=jnp.float32,
    )
    result = lax.psum_scatter(partial_value, "bulk", scatter_dimension=0, tiled=True)
    return result


def solution(mesh):
    in_specs = (P("blk", "bulk"), P("bulk", "blk"), P("bulk", None))
    out_specs = P("bulk", "blk")
    return jax.shard_map(
        on_device, mesh=mesh, in_specs=in_specs, out_specs=out_specs, check_vma=False
    )
```

profile of v0, /device:TPU:1, one launch (start us, length us, event | category | flops | bytes accessed | tf_op | source)
XLA Modules:
  0.0 634.6 jit_solution(16535322805359047024)
XLA Ops:
  6.5 0.0 all-gather.3.cloned.1.call-start
  6.5 0.7 all-gather.3.cloned.1.call-update
  7.3 0.0 all-reduce.3.cloned.1.call-start
  7.3 0.9 fusion.2
  8.2 0.1 broadcast_in_dim.3
  8.3 0.1 mul.10
  8.4 75.4 %all-gather.3.cloned.1.call-done = bf16[16,100,1800]{2,1,0:T(8,128)(2,1)} async-done(((bf16[1,100,1800]{2,1,0:T(8,128)(2,1)}), bf16[16,100,1800]{2,1,0:T(8,128)(2,1)}) %all-gather.3.cloned.1.call-update) | async-done | bytes 5760016 | tf_op jit(solution)/shard_map/all_gather | solution.py:13
  83.8 8.7 %reshape.6 = bf16[1600,1800]{1,0:T(8,128)(2,1)} reshape(bf16[16,100,1800]{2,1,0:T(8,128)(2,1)} %all-gather.3.cloned.1.call-done) | data formatting | bytes 11520000
  92.6 21.6 %convolution_bitcast_fusion = f32[1600,1800]{0,1:T(8,128)} fusion(bf16[1600,1800]{1,0:T(8,128)(2,1)} %reshape.6, bf16[1800,1800]{1,0:T(8,128)(2,1)} %param.4, f32[1800]{0:T(1024)S(1)} %mul.10), kind=kOutput, calls=%fused_computation.1 | convolution fusion | flops 10377719808 | bytes 23767200 | tf_op jit(solution)/shard_map/dot_general | solution.py:12
  114.1 0.0 copy-start
  114.1 0.0 all-reduce.3.cloned.1.call-update
  114.2 0.6 copy-done
  114.8 0.6 dynamic-slice
  116.1 508.6 %all-reduce.3.cloned.1.call-done = f32[1600,1800]{0,1:T(8,128)} async-done(((f32[1600,1800]{0,1:T(8,128)}), f32[1600,1800]{0,1:T(8,128)}) %all-reduce.3.cloned.1.call-update) | async-done | bytes 11520016
  624.7 1.8 constant_dynamic-slice_fusion
  626.5 1.2 copy.6
Async XLA Ops:
  6.5 77.3 %all-gather.3.cloned.1.call-start = ((), (), s32[]{:S(2)}) async-start(), calls=%async_computation | async-start | bytes 6789120 | tf_op jit(solution)/shard_map/all_gather | solution.py:13
  7.3 617.4 %all-reduce.3.cloned.1.call-start = ((), (), s32[]{:S(2)}) async-start(), calls=%async_computation.1 | async-start | bytes 23961600
  114.1 0.7 copy-start
Sparse Core Ops, SparseCore 0:
  10.0 73.7 all-gather.2
  114.3 510.3 all-reduce.2
where the time goes:
time: 636 us; the launch traced here: 635 us
  waiting for transfers between devices  585 us (92%)
  matrix products  21.6 us (3%)
  between operations  14.1 us (2%)
  local copies, waits for them, and re-layouts  13.2 us (2%)
    unnamed x3, waiting for transfers between devices  509 us
    all_gather x1, waiting for transfers between devices, on_device(): lax.all_gather(amplitudes, 'blk', axis=0, tiled=True)  75.4 us
    dot_general x1, matrix products, on_device(): jnp.dot(lax.all_gather(amplitudes, 'blk', axis=0, tiled=True), panel, pre...  21.6 us
  transfers between devices with their start and end apart: 2, of which 2 were waited for; matrix products, arithmetic and copies ran while one was open for 0% of the time, Pallas kernels for 0%

commit v1 on v0

v1 whole, which is shorter than its diff:
```python
import functools

import jax
import jax.numpy as jnp
from jax import lax
from jax.experimental import pallas as pl
from jax.experimental.pallas import tpu as pltpu
from jax.sharding import PartitionSpec as P

MESH = pl.DeviceIdType.MESH
F32 = jnp.float32

DELTA = (4, 3, 5, 2, 6, 1, 7, 0)
NZ = 4
NB = 7
NX = NB - NZ
XA = (NX + 1) // 2
LANES = 128
PAD = 112
ROWS = 104
HALVES = ((0, 64), (64, 48))


def kernel(a_ref, cd_ref, b_hbm, out_ref, abuf, b_ref, part, tmp, left, zs, zr, zsx, zrx, xs, xr, xsx, xrx,
           es, er, esx, erx, fs, fr, b_sem, g_send, g_recv, z_send, z_recv, x_send, x_recv, e_send, e_recv):
    rows, depth = a_ref.shape
    tail = b_hbm.shape[1] - NB * 256
    blk, bulk = lax.axis_index("blk"), lax.axis_index("bulk")
    y, h, k = blk // 4, (blk // 2) % 2, blk % 2
    z, xl = bulk // 2, bulk % 2

    def at_y(step):
        return (((y + step + 4) % 4) * 4 + h * 2 + k, bulk)

    def at_z(step):
        return (blk, ((z + step + 8) % 8) * 2 + xl)

    up, down = at_z(1), at_z(-1)
    y_up, y_down = at_y(1), at_y(-1)
    across = (y * 4 + (1 - h) * 2 + k, bulk)
    sibling = (y * 4 + h * 2 + (1 - k), bulk)
    pair = (blk, z * 2 + (1 - xl))

    b_copy = pltpu.make_async_copy(b_hbm, b_ref, b_sem)
    b_copy.start()

    barrier = pltpu.get_barrier_semaphore()
    partners = (up, down, y_up, y_down, across, sibling, pair)
    for partner in partners:
        pl.semaphore_signal(barrier, inc=1, device_id=partner, device_id_type=MESH)

    def remote(src, dst, send, recv, target):
        return pltpu.make_async_remote_copy(
            src_ref=src, dst_ref=dst, send_sem=send, recv_sem=recv, device_id=target, device_id_type=MESH
        )

    own = [(z + d) % 8 for d in DELTA]
    dys = [(y - c // 2 + 4) % 4 for c in own]
    sames = [h == c % 2 for c in own]
    sources = [jnp.logical_and(dy == 0, same) for dy, same in zip(dys, sames)]
    p_own = sum(jnp.where(s, p, 0) for p, s in enumerate(sources))

    per_block = depth // cd_ref.shape[0]
    column = lax.broadcasted_iota(jnp.int32, (1, depth), 1)
    weight = jnp.zeros((1, depth), F32)
    for block in range(cd_ref.shape[0]):
        factor = jnp.where(cd_ref[block, 0] == cd_ref[block, 1], 1.0, 2.0).astype(F32)
        inside = jnp.logical_and(column >= block * per_block, column < (block + 1) * per_block)
        weight = jnp.where(inside, factor, weight)
    abuf[p_own, k] = jnp.zeros((PAD, depth), jnp.bfloat16)
    abuf[p_own, k, 0:rows] = (a_ref[...].astype(F32) * weight).astype(jnp.bfloat16)
    tmp[...] = jnp.zeros_like(tmp)

    pl.semaphore_wait(barrier, len(partners))

    def half(p, l, part_of):
        start, size = HALVES[part_of]
        return abuf.at[p, l, pl.ds(start, size)]

    def g_copy(p, part_of, way, target):
        ref = half(p, k, part_of)
        return remote(ref, ref, g_send.at[p, part_of, way], g_recv.at[p, k, part_of], target)

    def g_sends(p, part_of):
        dy = dys[p]
        goes_up = jnp.logical_or(dy == 0, dy == 1) if part_of == 0 else dy == 0
        goes_down = jnp.logical_or(dy == 0, dy == 3) if part_of == 1 else dy == 0
        return (
            (sources[p], g_copy(p, part_of, 0, across)),
            (goes_up, g_copy(p, part_of, 1, y_up)),
            (goes_down, g_copy(p, part_of, 2, y_down)),
            (None, g_copy(p, part_of, 3, sibling)),
        )

    def pass_on(p, part_of):
        for when, copy in g_sends(p, part_of):
            if when is None:
                copy.start()
            else:
                pl.when(when)(copy.start)

    def launch(p):
        @pl.when(sources[p])
        def _():
            for part_of in range(2):
                for _, copy in g_sends(p, part_of):
                    copy.start()

    def arrive(p):
        @pl.when(jnp.logical_not(sources[p]))
        def _():
            for part_of in range(2):
                g_copy(p, part_of, 3, sibling).wait_recv()
                dy = dys[p]
                for when, copy in g_sends(p, part_of)[1:]:
                    if when is None:
                        copy.start()
                    else:
                        pl.when(when)(copy.start)

    def arrive_sibling(p):
        for part_of in range(2):
            ref = half(p, 1 - k, part_of)
            remote(ref, ref, g_send.at[p, part_of, 3], g_recv.at[p, 1 - k, part_of], sibling).wait_recv()

    def multiply(p):
        lhs = abuf[p].reshape(2 * PAD, depth)

        def body(nb, _):
            r = jnp.dot(lhs, b_ref[:, pl.ds(pl.multiple_of(nb * 256, 256), 256)], preferred_element_type=F32)
            for l in range(2):
                for side in range(2):
                    part[p, l, nb, side * ROWS:(side + 1) * ROWS] = r[
                        l * PAD:l * PAD + ROWS, side * LANES:(side + 1) * LANES]
            return 0

        lax.fori_loop(0, NB, body, 0)
        r = jnp.dot(lhs, b_ref[:, NB * 256:], preferred_element_type=F32)
        for l in range(2):
            tmp[0:PAD, 0:tail] = r[l * PAD:(l + 1) * PAD]
            left[p, l] = tmp[...].T[0:8]

    def add(p, l, first, count, q, scale):
        factor = scale[0:8]

        def body(b, _):
            more = q[b].astype(F32).reshape(-1, 8, LANES) * factor
            v = part[p, l, first + b].reshape(-1, 8, LANES) + more
            part[p, l, first + b] = v.reshape(2 * ROWS, LANES)
            return 0

        lax.fori_loop(0, count, body, 0)

    def quantize(p, l, first, count, q, scale):
        def largest(b, m):
            v = jnp.abs(part[p, l, first + b].reshape(-1, 8, LANES))
            return jnp.maximum(m, jnp.max(v, axis=0))

        m = lax.fori_loop(0, count, largest, jnp.zeros((8, LANES), F32))
        m = jnp.maximum(m, 1e-30)
        scale[0:8] = m * (1.0 / 32767.0)
        inverse = 32767.0 / m

        def body(b, _):
            v = part[p, l, first + b].reshape(-1, 8, LANES) * inverse
            q[b] = jnp.round(v).astype(jnp.int32).astype(jnp.int16).reshape(2 * ROWS, LANES)
            return 0

        lax.fori_loop(0, count, body, 0)

    started = []

    def send(copies):
        for copy in copies:
            copy.start()
            started.append(copy)

    def z_copies(way, s, l):
        target = up if way == 0 else down
        return (
            remote(zsx.at[way, s, l], zrx.at[way, s, l], z_send.at[way, s, l, 0], z_recv.at[way, s, l, 0], target),
            remote(zs.at[way, s, l], zr.at[way, s, l], z_send.at[way, s, l, 1], z_recv.at[way, s, l, 1], target),
        )

    def x_copies(way, s):
        target = up if way == 0 else down
        if s == 0:
            blocks = pl.ds(0, XA) if way == 0 else pl.ds(XA, NX - XA)
        else:
            blocks = pl.ds(0, NX)
        return (
            remote(xsx.at[way, s], xrx.at[way, s], x_send.at[way, s, 0], x_recv.at[way, s, 0], target),
            remote(xs.at[way, s, blocks], xr.at[way, s, blocks], x_send.at[way, s, 1], x_recv.at[way, s, 1], target),
        )

    def e_copies(p):
        q, r = (es.at[p], er.at[p]) if p < 8 else (fs, fr)
        return (
            remote(esx.at[p], erx.at[p], e_send.at[p, 0], e_recv.at[p, 0], pair),
            remote(q, r, e_send.at[p, 1], e_recv.at[p, 1], pair),
        )

    def receive(copies):
        for copy in copies:
            copy.wait_recv()

    def z_receive(p, way, s, l):
        receive(z_copies(way, s, l))
        add(p, l, 0, NZ, zr.at[way, s, l], zrx.at[way, s, l])
        left[p, l] = left[p, l] + zrx[way, s, l, 8:16]

    def z_emit(p, way, s, l):
        quantize(p, l, 0, NZ, zs.at[way, s, l], zsx.at[way, s, l])
        zsx[way, s, l, 8:16] = left[p, l]
        send(z_copies(way, s, l))

    def x_receive(p, way, s):
        receive(x_copies(way, s))
        first, count = (0, NX) if s > 0 else ((0, XA) if way == 0 else (XA, NX - XA))
        add(p, xl, NZ + first, count, xr.at[way, s, pl.ds(first, count)], xrx.at[way, s])

    def x_emit(p, way, s):
        first, count = (0, NX) if s > 0 else ((0, XA) if way == 0 else (XA, NX - XA))
        quantize(p, xl, NZ + first, count, xs.at[way, s, pl.ds(first, count)], xsx.at[way, s])
        send(x_copies(way, s))

    def e_emit(p):
        quantize(p, 1 - xl, NZ, NX, es.at[p], esx.at[p])
        send(e_copies(p))

    def e_receive(p):
        receive(e_copies(p))
        add(p, xl, NZ, NX, er.at[p], erx.at[p])

    for p in (0, 1, 2):
        launch(p)
    arrive(0)
    launch(3)
    launch(4)
    arrive_sibling(0)
    b_copy.wait()
    multiply(0)
    e_emit(0)
    z_emit(0, 0, 0, 0)
    z_emit(0, 1, 0, 1)

    for s in (1, 2, 3, 4):
        now = (2 * s - 1, 2 * s) if s < 4 else (7,)
        for p in now:
            arrive(p)
        for p in (2 * s + 3, 2 * s + 4):
            if 4 < p < 8:
                launch(p)
        for p in now:
            arrive_sibling(p)
            multiply(p)
            e_emit(p)
        before = (2 * s - 3, 2 * s - 2) if s > 1 else (0, 0)
        if s == 1:
            e_receive(0)
            x_emit(0, 0, 0)
            x_emit(0, 1, 0)
        else:
            for way in (0, 1):
                p = before[way]
                e_receive(p)
                x_receive(p, way, s - 2)
                x_emit(p, way, s - 1)
        if s < 4:
            for way in (0, 1):
                p = now[way]
                for l in (way, 1 - way):
                    if s > 1 or l == way:
                        z_receive(p, way, s - 1, l)
                    z_emit(p, way, s, l)

    for way in (0, 1):
        z_receive(7, way, 3, 1 - xl)
    quantize(7, 1 - xl, 0, NZ, fs, esx.at[8])
    esx[8, 8:16] = left[7, 1 - xl]
    send(e_copies(8))
    for way in (0, 1):
        z_receive(7, way, 3, xl)
    e_receive(7)
    for way in (0, 1):
        x_receive(7, way, 3)

    def write(b):
        for side in range(2):
            out_ref[:, (2 * b + side) * LANES:(2 * b + side + 1) * LANES] = part[
                7, xl, b, side * ROWS:side * ROWS + rows]

    for b in range(NZ, NB):
        write(b)
    receive(e_copies(8))
    add(7, xl, 0, NZ, fr, erx.at[8])
    for b in range(NZ):
        write(b)
    tmp[0:8] = left[7, xl] + erx[8, 8:16]
    out_ref[:, NB * 256:] = tmp[...].T[0:rows, 0:tail]

    for p in range(8):
        for part_of in range(2):
            for when, copy in g_sends(p, part_of):
                if when is None:
                    copy.wait_send()
                else:
                    pl.when(when)(copy.wait_send)
    for copy in started:
        copy.wait_send()


def on_device(amplitudes, integrals, cd_blocks):
    rows, depth = amplitudes.shape
    width = integrals.shape[1]
    message = (2 * ROWS, LANES)
    dma = pltpu.SemaphoreType.DMA
    return pl.pallas_call(
        kernel,
        out_shape=jax.ShapeDtypeStruct((rows, width), F32),
        in_specs=[
            pl.BlockSpec(memory_space=pltpu.VMEM),
            pl.BlockSpec(memory_space=pltpu.SMEM),
            pl.BlockSpec(memory_space=pl.ANY),
        ],
        out_specs=pl.BlockSpec(memory_space=pltpu.VMEM),
        scratch_shapes=[
            pltpu.VMEM((8, 2, PAD, depth), jnp.bfloat16),
            pltpu.VMEM((depth, width), jnp.bfloat16),
            pltpu.VMEM((8, 2, NB) + message, F32),
            pltpu.VMEM((LANES, LANES), F32),
            pltpu.VMEM((8, 2, 8, LANES), F32),
            pltpu.VMEM((2, 4, 2, NZ) + message, jnp.int16),
            pltpu.VMEM((2, 4, 2, NZ) + message, jnp.int16),
            pltpu.VMEM((2, 4, 2, 16, LANES), F32),
            pltpu.VMEM((2, 4, 2, 16, LANES), F32),
            pltpu.VMEM((2, 4, NX) + message, jnp.int16),
            pltpu.VMEM((2, 4, NX) + message, jnp.int16),
            pltpu.VMEM((2, 4, 8, LANES), F32),
            pltpu.VMEM((2, 4, 8, LANES), F32),
            pltpu.VMEM((8, NX) + message, jnp.int16),
            pltpu.VMEM((8, NX) + message, jnp.int16),
            pltpu.VMEM((9, 16, LANES), F32),
            pltpu.VMEM((9, 16, LANES), F32),
            pltpu.VMEM((NZ,) + message, jnp.int16),
            pltpu.VMEM((NZ,) + message, jnp.int16),
            dma(()),
            dma((8, 2, 4)),
            dma((8, 2, 2)),
            dma((2, 4, 2, 2)),
            dma((2, 4, 2, 2)),
            dma((2, 4, 2)),
            dma((2, 4, 2)),
            dma((9, 2)),
            dma((9, 2)),
        ],
        compiler_params=pltpu.CompilerParams(
            collective_id=0, has_side_effects=True, vmem_limit_bytes=56 * 2**20
        ),
    )(amplitudes, cd_blocks, integrals)


def solution(mesh):
    return jax.shard_map(
        on_device,
        mesh=mesh,
        in_specs=(P("blk", "bulk"), P("bulk", "blk"), P("bulk", None)),
        out_specs=P("bulk", "blk"),
        check_vma=False,
    )
```

time: 636 us -> 136 us (0.21)
  the two profiles are of different devices: /device:TPU:1 before, /device:TPU:17 now
where the time goes in v1:
time: 136 us
  Pallas kernels  134 us (99%)
  local copies, waits for them, and re-layouts  2.07 us (2%)
    pallas_call x1, Pallas kernels, on_device(): pl.pallas_call(kernel, out_shape=jax.ShapeDtypeStruct((rows, width), F32)...  134 us

profile of v1, /device:TPU:17, one launch (start us, length us, event | category | flops | bytes accessed | tf_op | source)
XLA Modules:
  0.0 135.7 jit_solution(8859953573552228712)
XLA Ops:
  0.0 133.7 %shard_map.37 = f32[100,1800]{1,0:T(8,128)} custom-call(bf16[100,1800]{1,0:T(8,128)(2,1)} %a_ref.1, s32[2,2]{1,0:T(2,128)} %cd_ref.1, bf16[1800,1800]{1,0:T(8,128)(2,1)} %b_hbm.1), custom_call_target="tpu_custom_call" | custom-call | tf_op jit(solution)/shard_map/pallas_call | solution.py:318
  133.7 2.1 %copy.5 = f32[100,1800]{1,0:T(8,128)} copy(f32[100,1800]{1,0:T(8,128)} %shard_map.37) | data formatting | bytes 1440000

commit v2 on v1

--- a/solution.py
+++ b/solution.py
@@ -11,20 +11,24 @@
 F32 = jnp.float32
 
 DELTA = (4, 3, 5, 2, 6, 1, 7, 0)
-NZ = 4
+NZ = 2
 NB = 7
 NX = NB - NZ
 XA = (NX + 1) // 2
 LANES = 128
 PAD = 112
 ROWS = 104
-HALVES = ((0, 64), (64, 48))
-
-
-def kernel(a_ref, cd_ref, b_hbm, out_ref, abuf, b_ref, part, tmp, left, zs, zr, zsx, zrx, xs, xr, xsx, xrx,
+FULL = 96
+QUAD = 512
+OWN, Y_M, Y_P, Y_2, R_OWN, R_M, R_P, R_2 = range(8)
+LAST = 8
+EARLY = (OWN, Y_M, Y_P)
+
+
+def kernel(a_ref, cd_ref, b_hbm, out_ref, abuf, ebuf, b_ref, part, tmp, left, zs, zr, zsx, zrx, xs, xr, xsx, xrx,
            es, er, esx, erx, fs, fr, b_sem, g_send, g_recv, z_send, z_recv, x_send, x_recv, e_send, e_recv):
     rows, depth = a_ref.shape
-    tail = b_hbm.shape[1] - NB * 256
+    tail = b_hbm.shape[1] - 2 * NB * LANES
     blk, bulk = lax.axis_index("blk"), lax.axis_index("bulk")
     y, h, k = blk // 4, (blk // 2) % 2, blk % 2
     z, xl = bulk // 2, bulk % 2
@@ -54,11 +58,12 @@
             src_ref=src, dst_ref=dst, send_sem=send, recv_sem=recv, device_id=target, device_id_type=MESH
         )
 
-    own = [(z + d) % 8 for d in DELTA]
-    dys = [(y - c // 2 + 4) % 4 for c in own]
-    sames = [h == c % 2 for c in own]
-    sources = [jnp.logical_and(dy == 0, same) for dy, same in zip(dys, sames)]
-    p_own = sum(jnp.where(s, p, 0) for p, s in enumerate(sources))
+    def place(n):
+        source = ((y + (0, -1, 1, 2)[n % 4] + 4) % 4) * 2 + (h if n < 4 else 1 - h)
+        d = (source - z + 8) % 8
+        return jnp.where(d < 4, 7 - 2 * d, 2 * (d - 4))
+
+    places = [place(n) for n in range(8)]
 
     per_block = depth // cd_ref.shape[0]
     column = lax.broadcasted_iota(jnp.int32, (1, depth), 1)
@@ -67,75 +72,74 @@
         factor = jnp.where(cd_ref[block, 0] == cd_ref[block, 1], 1.0, 2.0).astype(F32)
         inside = jnp.logical_and(column >= block * per_block, column < (block + 1) * per_block)
         weight = jnp.where(inside, factor, weight)
-    abuf[p_own, k] = jnp.zeros((PAD, depth), jnp.bfloat16)
-    abuf[p_own, k, 0:rows] = (a_ref[...].astype(F32) * weight).astype(jnp.bfloat16)
     tmp[...] = jnp.zeros_like(tmp)
+    weighted = a_ref[...].astype(F32) * weight
+    main = 2 * NB * LANES
+    abuf[OWN, k, 0:FULL, 0:main] = weighted[0:FULL, 0:main].astype(jnp.bfloat16)
+    tmp[0:rows, 0:depth - main] = weighted[:, main:]
+    ends = tmp[...].T[0:8]
+    last = weighted[FULL:rows, 0:main]
+    spare = jnp.concatenate([last[:, 3 * QUAD:], ends[0:4], ends[4:8]], axis=1)
+    ebuf[OWN, k] = jnp.concatenate(
+        [last[:, 0:QUAD], last[:, QUAD:2 * QUAD], last[:, 2 * QUAD:3 * QUAD], spare], axis=0).astype(jnp.bfloat16)
+    tmp[...] = jnp.zeros_like(tmp)
 
     pl.semaphore_wait(barrier, len(partners))
 
-    def half(p, l, part_of):
-        start, size = HALVES[part_of]
-        return abuf.at[p, l, pl.ds(start, size)]
-
-    def g_copy(p, part_of, way, target):
-        ref = half(p, k, part_of)
-        return remote(ref, ref, g_send.at[p, part_of, way], g_recv.at[p, k, part_of], target)
-
-    def g_sends(p, part_of):
-        dy = dys[p]
-        goes_up = jnp.logical_or(dy == 0, dy == 1) if part_of == 0 else dy == 0
-        goes_down = jnp.logical_or(dy == 0, dy == 3) if part_of == 1 else dy == 0
-        return (
-            (sources[p], g_copy(p, part_of, 0, across)),
-            (goes_up, g_copy(p, part_of, 1, y_up)),
-            (goes_down, g_copy(p, part_of, 2, y_down)),
-            (None, g_copy(p, part_of, 3, sibling)),
-        )
-
-    def pass_on(p, part_of):
-        for when, copy in g_sends(p, part_of):
-            if when is None:
-                copy.start()
-            else:
-                pl.when(when)(copy.start)
-
-    def launch(p):
-        @pl.when(sources[p])
-        def _():
-            for part_of in range(2):
-                for _, copy in g_sends(p, part_of):
-                    copy.start()
-
-    def arrive(p):
-        @pl.when(jnp.logical_not(sources[p]))
-        def _():
-            for part_of in range(2):
-                g_copy(p, part_of, 3, sibling).wait_recv()
-                dy = dys[p]
-                for when, copy in g_sends(p, part_of)[1:]:
-                    if when is None:
-                        copy.start()
-                    else:
-                        pl.when(when)(copy.start)
-
-    def arrive_sibling(p):
-        for part_of in range(2):
-            ref = half(p, 1 - k, part_of)
-            remote(ref, ref, g_send.at[p, part_of, 3], g_recv.at[p, 1 - k, part_of], sibling).wait_recv()
-
-    def multiply(p):
-        lhs = abuf[p].reshape(2 * PAD, depth)
-
-        def body(nb, _):
-            r = jnp.dot(lhs, b_ref[:, pl.ds(pl.multiple_of(nb * 256, 256), 256)], preferred_element_type=F32)
+    def half(n, l, part_of):
+        if part_of == 2:
+            return ebuf.at[n, l]
+        return abuf.at[n, l, pl.ds(part_of * (FULL // 2), FULL // 2), pl.ds(0, main)]
+
+    started = []
+
+    def send(copies):
+        for copy in copies:
+            copy.start()
+            started.append(copy)
+
+    def give(source, target_slot, part_of, target):
+        send([remote(half(source, k, part_of), half(target_slot, k, part_of), g_send.at[target_slot, part_of, 0],
+                     g_recv.at[target_slot, k, part_of], target)])
+
+    def share(n, part_of):
+        ref = half(n, k, part_of)
+        send([remote(ref, ref, g_send.at[n, part_of, 1], g_recv.at[n, k, part_of], sibling)])
+
+    def arrive(n, part_of):
+        ref = half(n, k, part_of)
+        remote(ref, ref, g_send.at[n, part_of, 0], g_recv.at[n, k, part_of], sibling).wait_recv()
+        share(n, part_of)
+
+    def arrive_sibling(n):
+        for part_of in range(3):
+            ref = half(n, 1 - k, part_of)
+            remote(ref, ref, g_send.at[n, part_of, 1], g_recv.at[n, 1 - k, part_of], sibling).wait_recv()
+
+    def unpack(n):
+        for l in range(2):
+            e = ebuf[n, l].astype(F32)
+            low = jnp.concatenate([e[0:4], e[4:8], e[8:12], e[12:16, 0:main - 3 * QUAD]], axis=1)
+            low = jnp.concatenate([low, jnp.zeros((PAD - FULL - 4, main), F32)], axis=0)
+            abuf[n, l, FULL:PAD, 0:main] = low.astype(jnp.bfloat16)
+            ends = jnp.concatenate([e[12:16, QUAD - 2 * LANES:QUAD - LANES], e[12:16, QUAD - LANES:]], axis=0)
+            abuf[n, l, :, main:] = ends.T[0:PAD].astype(jnp.bfloat16)
+
+    def multiply(n, p):
+        unpack(n)
+        lhs = abuf[n].reshape(2 * PAD, depth)
+        wide = NB * LANES
+
+        def body(side, _):
+            r = jnp.dot(lhs, b_ref[:, pl.ds(pl.multiple_of(side * wide, LANES), wide)], preferred_element_type=F32)
             for l in range(2):
-                for side in range(2):
-                    part[p, l, nb, side * ROWS:(side + 1) * ROWS] = r[
-                        l * PAD:l * PAD + ROWS, side * LANES:(side + 1) * LANES]
+                for b in range(NB):
+                    part[p, l, b, pl.ds(pl.multiple_of(side * ROWS, 8), ROWS)] = r[
+                        l * PAD:l * PAD + ROWS, b * LANES:(b + 1) * LANES]
             return 0
 
-        lax.fori_loop(0, NB, body, 0)
-        r = jnp.dot(lhs, b_ref[:, NB * 256:], preferred_element_type=F32)
+        lax.fori_loop(0, 2, body, 0)
+        r = jnp.dot(lhs, b_ref[:, 2 * wide:], preferred_element_type=F32)
         for l in range(2):
             tmp[0:PAD, 0:tail] = r[l * PAD:(l + 1) * PAD]
             left[p, l] = tmp[...].T[0:8]
@@ -167,13 +171,6 @@
             return 0
 
         lax.fori_loop(0, count, body, 0)
-
-    started = []
-
-    def send(copies):
-        for copy in copies:
-            copy.start()
-            started.append(copy)
 
     def z_copies(way, s, l):
         target = up if way == 0 else down
@@ -194,7 +191,7 @@
         )
 
     def e_copies(p):
-        q, r = (es.at[p], er.at[p]) if p < 8 else (fs, fr)
+        q, r = (fs, fr) if p is LAST else (es.at[p], er.at[p])
         return (
             remote(esx.at[p], erx.at[p], e_send.at[p, 0], e_recv.at[p, 0], pair),
             remote(q, r, e_send.at[p, 1], e_recv.at[p, 1], pair),
@@ -232,53 +229,107 @@
         receive(e_copies(p))
         add(p, xl, NZ, NX, er.at[p], erx.at[p])
 
-    for p in (0, 1, 2):
-        launch(p)
-    arrive(0)
-    launch(3)
-    launch(4)
-    arrive_sibling(0)
+    for part_of in range(3):
+        give(OWN, Y_M, part_of, y_up)
+        give(OWN, Y_P, part_of, y_down)
+        give(OWN, R_OWN, part_of, across)
+        share(OWN, part_of)
     b_copy.wait()
-    multiply(0)
-    e_emit(0)
-    z_emit(0, 0, 0, 0)
-    z_emit(0, 1, 0, 1)
-
-    for s in (1, 2, 3, 4):
-        now = (2 * s - 1, 2 * s) if s < 4 else (7,)
-        for p in now:
-            arrive(p)
-        for p in (2 * s + 3, 2 * s + 4):
-            if 4 < p < 8:
-                launch(p)
-        for p in now:
-            arrive_sibling(p)
-            multiply(p)
-            e_emit(p)
-        before = (2 * s - 3, 2 * s - 2) if s > 1 else (0, 0)
-        if s == 1:
+    arrive_sibling(OWN)
+    multiply(OWN, places[OWN])
+    arrive(Y_M, 0)
+    give(Y_M, Y_2, 0, y_up)
+    arrive(Y_P, 0)
+    arrive(R_OWN, 0)
+    give(R_OWN, R_M, 0, y_up)
+    give(R_OWN, R_P, 0, y_down)
+    for part_of in (1, 2):
+        arrive(Y_P, part_of)
+        give(Y_P, Y_2, part_of, y_down)
+    for part_of in (1, 2):
+        arrive(R_OWN, part_of)
+        give(R_OWN, R_M, part_of, y_up)
+        give(R_OWN, R_P, part_of, y_down)
+    for part_of in (1, 2):
+        arrive(Y_M, part_of)
+    e_emit(places[OWN])
+    for n in (Y_M, Y_P):
+        arrive_sibling(n)
+        multiply(n, places[n])
+    for part_of in range(3):
+        arrive(Y_2, part_of)
+        give(Y_2, R_2, part_of, across)
+    e_emit(places[Y_M])
+    e_emit(places[Y_P])
+    for n in (R_OWN, Y_2):
+        arrive_sibling(n)
+        multiply(n, places[n])
+    for n in (R_M, R_P, R_2):
+        for part_of in range(3):
+            arrive(n, part_of)
+    for n in (R_M, R_P, R_2):
+        arrive_sibling(n)
+    keys = [places[n] * 8 + n for n in (R_M, R_P, R_2)]
+    low, high = jnp.minimum(keys[0], keys[1]), jnp.maximum(keys[0], keys[1])
+    first, second = jnp.minimum(low, keys[2]), jnp.maximum(low, jnp.minimum(high, keys[2]))
+    third = jnp.maximum(high, keys[2])
+
+    def e_late(p):
+        early = [places[n] == p for n in EARLY]
+        done = functools.reduce(jnp.logical_or, early)
+
+        @pl.when(jnp.logical_not(done))
+        def _():
+            quantize(p, 1 - xl, NZ, NX, es.at[p], esx.at[p])
+            for copy in e_copies(p):
+                copy.start()
+
+        late.append((done, p))
+
+    late = []
+    chunks = ((0, 0), (1, 2), (3, 4), (5, 6))
+
+    def z_part(s, way, l):
+        p = chunks[s][way]
+        if s > 1 or (s == 1 and l == way):
+            z_receive(p, way, s - 1, l)
+        z_emit(p, way, s, l)
+
+    def x_step(s):
+        if s == 0:
             e_receive(0)
-            x_emit(0, 0, 0)
-            x_emit(0, 1, 0)
-        else:
+        for way in (0, 1):
+            p = chunks[s][way]
+            if s > 0:
+                e_receive(p)
+                x_receive(p, way, s - 1)
+            x_emit(p, way, s)
+
+    multiply(first % 8, first // 8)
+    e_late(0)
+    z_part(0, 0, 0)
+    z_part(0, 1, 1)
+    multiply(second % 8, second // 8)
+    z_part(1, 0, 1)
+    multiply(third % 8, third // 8)
+    z_part(1, 1, 0)
+    for p in range(1, 8):
+        e_late(p)
+    z_part(1, 0, 0)
+    z_part(1, 1, 1)
+    x_step(0)
+    for s in (2, 3):
+        for l in range(2):
             for way in (0, 1):
-                p = before[way]
-                e_receive(p)
-                x_receive(p, way, s - 2)
-                x_emit(p, way, s - 1)
-        if s < 4:
-            for way in (0, 1):
-                p = now[way]
-                for l in (way, 1 - way):
-                    if s > 1 or l == way:
-                        z_receive(p, way, s - 1, l)
-                    z_emit(p, way, s, l)
+                z_part(s, way, l)
+        x_step(s - 1)
+    x_step(3)
 
     for way in (0, 1):
         z_receive(7, way, 3, 1 - xl)
-    quantize(7, 1 - xl, 0, NZ, fs, esx.at[8])
-    esx[8, 8:16] = left[7, 1 - xl]
-    send(e_copies(8))
+    quantize(7, 1 - xl, 0, NZ, fs, esx.at[LAST])
+    esx[LAST, 8:16] = left[7, 1 - xl]
+    send(e_copies(LAST))
     for way in (0, 1):
         z_receive(7, way, 3, xl)
     e_receive(7)
@@ -287,25 +338,23 @@
 
     def write(b):
         for side in range(2):
-            out_ref[:, (2 * b + side) * LANES:(2 * b + side + 1) * LANES] = part[
-                7, xl, b, side * ROWS:side * ROWS + rows]
+            first = (side * NB + b) * LANES
+            out_ref[:, first:first + LANES] = part[7, xl, b, side * ROWS:side * ROWS + rows]
 
     for b in range(NZ, NB):
         write(b)
-    receive(e_copies(8))
-    add(7, xl, 0, NZ, fr, erx.at[8])
+    receive(e_copies(LAST))
+    add(7, xl, 0, NZ, fr, erx.at[LAST])
     for b in range(NZ):
         write(b)
-    tmp[0:8] = left[7, xl] + erx[8, 8:16]
-    out_ref[:, NB * 256:] = tmp[...].T[0:rows, 0:tail]
-
-    for p in range(8):
-        for part_of in range(2):
-            for when, copy in g_sends(p, part_of):
-                if when is None:
-                    copy.wait_send()
-                else:
-                    pl.when(when)(copy.wait_send)
+    tmp[0:8] = left[7, xl] + erx[LAST, 8:16]
+    out_ref[:, 2 * NB * LANES:] = tmp[...].T[0:rows, 0:tail]
+
+    for done, p in late:
+        @pl.when(jnp.logical_not(done))
+        def _(p=p):
+            for copy in e_copies(p):
+                copy.wait_send()
     for copy in started:
         copy.wait_send()
 
@@ -326,6 +375,7 @@
         out_specs=pl.BlockSpec(memory_space=pltpu.VMEM),
         scratch_shapes=[
             pltpu.VMEM((8, 2, PAD, depth), jnp.bfloat16),
+            pltpu.VMEM((8, 2, 16, QUAD), jnp.bfloat16),
             pltpu.VMEM((depth, width), jnp.bfloat16),
             pltpu.VMEM((8, 2, NB) + message, F32),
             pltpu.VMEM((LANES, LANES), F32),
@@ -345,8 +395,8 @@
             pltpu.VMEM((NZ,) + message, jnp.int16),
             pltpu.VMEM((NZ,) + message, jnp.int16),
             dma(()),
-            dma((8, 2, 4)),
-            dma((8, 2, 2)),
+            dma((8, 3, 2)),
+            dma((8, 2, 3)),
             dma((2, 4, 2, 2)),
             dma((2, 4, 2, 2)),
             dma((2, 4, 2)),

time: 136 us -> 95.2 us (0.70)
  the two profiles are of different devices: /device:TPU:17 before, /device:TPU:1 now
where the time goes in v2:
time: 95.2 us; the launch traced here: 95.1 us
  Pallas kernels  93 us (98%)
  local copies, waits for them, and re-layouts  2.07 us (2%)
    pallas_call x1, Pallas kernels, on_device(): pl.pallas_call(kernel, out_shape=jax.ShapeDtypeStruct((rows, width), F32)...  93 us
    unnamed x1, local copies, waits for them, and re-layouts  2.07 us

profile of v2, /device:TPU:1, one launch (start us, length us, event | category | flops | bytes accessed | tf_op | source)
XLA Modules:
  0.0 95.1 jit_solution(14252018114615675283)
XLA Ops:
  0.0 93.0 %shard_map.37 = f32[100,1800]{1,0:T(8,128)} custom-call(bf16[100,1800]{1,0:T(8,128)(2,1)} %a_ref.1, s32[2,2]{1,0:T(2,128)} %cd_ref.1, bf16[1800,1800]{1,0:T(8,128)(2,1)} %b_hbm.1), custom_call_target="tpu_custom_call" | custom-call | tf_op jit(solution)/shard_map/pallas_call | solution.py:367
  93.0 2.1 %copy.5 = f32[100,1800]{1,0:T(8,128)} copy(f32[100,1800]{1,0:T(8,128)} %shard_map.37) | data formatting | bytes 1440000

commit v3 on v2

--- a/solution.py
+++ b/solution.py
@@ -11,7 +11,7 @@
 F32 = jnp.float32
 
 DELTA = (4, 3, 5, 2, 6, 1, 7, 0)
-NZ = 2
+NZ = 3
 NB = 7
 NX = NB - NZ
 XA = (NX + 1) // 2
@@ -22,7 +22,7 @@
 QUAD = 512
 OWN, Y_M, Y_P, Y_2, R_OWN, R_M, R_P, R_2 = range(8)
 LAST = 8
-EARLY = (OWN, Y_M, Y_P)
+EARLY = (OWN, Y_M, Y_P, R_OWN, Y_2)
 
 
 def kernel(a_ref, cd_ref, b_hbm, out_ref, abuf, ebuf, b_ref, part, tmp, left, zs, zr, zsx, zrx, xs, xr, xsx, xrx,
@@ -125,21 +125,24 @@
             ends = jnp.concatenate([e[12:16, QUAD - 2 * LANES:QUAD - LANES], e[12:16, QUAD - LANES:]], axis=0)
             abuf[n, l, :, main:] = ends.T[0:PAD].astype(jnp.bfloat16)
 
-    def multiply(n, p):
-        unpack(n)
+    def multiply(n, p, sides=(0, 2)):
         lhs = abuf[n].reshape(2 * PAD, depth)
         wide = NB * LANES
 
         def body(side, _):
             r = jnp.dot(lhs, b_ref[:, pl.ds(pl.multiple_of(side * wide, LANES), wide)], preferred_element_type=F32)
             for l in range(2):
-                for b in range(NB):
-                    part[p, l, b, pl.ds(pl.multiple_of(side * ROWS, 8), ROWS)] = r[
-                        l * PAD:l * PAD + ROWS, b * LANES:(b + 1) * LANES]
+                for j in range(NB):
+                    tile = side * NB + j
+                    part[p, l, tile // 2, pl.ds(pl.multiple_of(tile % 2 * ROWS, 8), ROWS)] = r[
+                        l * PAD:l * PAD + ROWS, j * LANES:(j + 1) * LANES]
             return 0
 
-        lax.fori_loop(0, 2, body, 0)
-        r = jnp.dot(lhs, b_ref[:, 2 * wide:], preferred_element_type=F32)
+        lax.fori_loop(sides[0], sides[1], body, 0)
+
+    def prepare(n, p):
+        unpack(n)
+        r = jnp.dot(abuf[n].reshape(2 * PAD, depth), b_ref[:, main:], preferred_element_type=F32)
         for l in range(2):
             tmp[0:PAD, 0:tail] = r[l * PAD:(l + 1) * PAD]
             left[p, l] = tmp[...].T[0:8]
@@ -206,11 +209,6 @@
         add(p, l, 0, NZ, zr.at[way, s, l], zrx.at[way, s, l])
         left[p, l] = left[p, l] + zrx[way, s, l, 8:16]
 
-    def z_emit(p, way, s, l):
-        quantize(p, l, 0, NZ, zs.at[way, s, l], zsx.at[way, s, l])
-        zsx[way, s, l, 8:16] = left[p, l]
-        send(z_copies(way, s, l))
-
     def x_receive(p, way, s):
         receive(x_copies(way, s))
         first, count = (0, NX) if s > 0 else ((0, XA) if way == 0 else (XA, NX - XA))
@@ -229,50 +227,85 @@
         receive(e_copies(p))
         add(p, xl, NZ, NX, er.at[p], erx.at[p])
 
+    chunks = ((0, 0), (1, 2), (3, 4), (5, 6))
+
+
+    def z_part(s, way, l):
+        p = chunks[s][way]
+
+        if s > 1 or (s == 1 and l == way):
+            z_receive(p, way, s - 1, l)
+        quantize(p, l, 0, NZ, zs.at[way, s, l], zsx.at[way, s, l])
+        zsx[way, s, l, 8:16] = left[p, l]
+        for copy in z_copies(way, s, l):
+            copy.start()
+
+    def give_all(source, slot, order, target):
+        for part_of in order:
+            give(source, slot, part_of, target)
+
+    rising, falling = (0, 1, 2), (2, 1, 0)
+    for i in range(3):
+        give(OWN, Y_M, rising[i], y_up)
+        give(OWN, Y_P, falling[i], y_down)
+        give(OWN, R_OWN, rising[i], across)
     for part_of in range(3):
-        give(OWN, Y_M, part_of, y_up)
-        give(OWN, Y_P, part_of, y_down)
-        give(OWN, R_OWN, part_of, across)
         share(OWN, part_of)
     b_copy.wait()
     arrive_sibling(OWN)
+    prepare(OWN, places[OWN])
     multiply(OWN, places[OWN])
+    e_emit(places[OWN])
     arrive(Y_M, 0)
     give(Y_M, Y_2, 0, y_up)
-    arrive(Y_P, 0)
+    for part_of in (2, 1):
+        arrive(Y_P, part_of)
+        give(Y_P, Y_2, part_of, y_down)
     arrive(R_OWN, 0)
     give(R_OWN, R_M, 0, y_up)
+    for part_of in (2, 1):
+        arrive(R_OWN, part_of)
+        give(R_OWN, R_P, part_of, y_down)
+    give_all(R_OWN, R_M, (1, 2), y_up)
     give(R_OWN, R_P, 0, y_down)
     for part_of in (1, 2):
-        arrive(Y_P, part_of)
-        give(Y_P, Y_2, part_of, y_down)
-    for part_of in (1, 2):
-        arrive(R_OWN, part_of)
-        give(R_OWN, R_M, part_of, y_up)
-        give(R_OWN, R_P, part_of, y_down)
-    for part_of in (1, 2):
         arrive(Y_M, part_of)
-    e_emit(places[OWN])
-    for n in (Y_M, Y_P):
-        arrive_sibling(n)
-        multiply(n, places[n])
+    arrive(Y_P, 0)
+    arrive_sibling(Y_M)
+    prepare(Y_M, places[Y_M])
+    multiply(Y_M, places[Y_M])
     for part_of in range(3):
         arrive(Y_2, part_of)
-        give(Y_2, R_2, part_of, across)
     e_emit(places[Y_M])
+    arrive_sibling(Y_P)
+    prepare(Y_P, places[Y_P])
+    multiply(Y_P, places[Y_P])
+    arrive(R_M, 0)
+    give(R_M, R_2, 0, y_up)
+    for part_of in (2, 1):
+        arrive(R_P, part_of)
+        give(R_P, R_2, part_of, y_down)
     e_emit(places[Y_P])
-    for n in (R_OWN, Y_2):
-        arrive_sibling(n)
-        multiply(n, places[n])
-    for n in (R_M, R_P, R_2):
-        for part_of in range(3):
-            arrive(n, part_of)
-    for n in (R_M, R_P, R_2):
-        arrive_sibling(n)
-    keys = [places[n] * 8 + n for n in (R_M, R_P, R_2)]
-    low, high = jnp.minimum(keys[0], keys[1]), jnp.maximum(keys[0], keys[1])
-    first, second = jnp.minimum(low, keys[2]), jnp.maximum(low, jnp.minimum(high, keys[2]))
-    third = jnp.maximum(high, keys[2])
+    arrive_sibling(R_OWN)
+    prepare(R_OWN, places[R_OWN])
+    multiply(R_OWN, places[R_OWN])
+    e_emit(places[R_OWN])
+    for part_of in (1, 2):
+        arrive(R_M, part_of)
+    arrive(R_P, 0)
+    arrive_sibling(Y_2)
+    prepare(Y_2, places[Y_2])
+    multiply(Y_2, places[Y_2])
+    e_emit(places[Y_2])
+    arrive_sibling(R_M)
+    prepare(R_M, places[R_M])
+    multiply(R_M, places[R_M])
+    for part_of in range(3):
+        arrive(R_2, part_of)
+    arrive_sibling(R_P)
+    arrive_sibling(R_2)
+    keys = [places[n] * 8 + n for n in (R_P, R_2)]
+    first, second = jnp.minimum(keys[0], keys[1]), jnp.maximum(keys[0], keys[1])
 
     def e_late(p):
         early = [places[n] == p for n in EARLY]
@@ -287,13 +320,6 @@
         late.append((done, p))
 
     late = []
-    chunks = ((0, 0), (1, 2), (3, 4), (5, 6))
-
-    def z_part(s, way, l):
-        p = chunks[s][way]
-        if s > 1 or (s == 1 and l == way):
-            z_receive(p, way, s - 1, l)
-        z_emit(p, way, s, l)
 
     def x_step(s):
         if s == 0:
@@ -305,24 +331,31 @@
                 x_receive(p, way, s - 1)
             x_emit(p, way, s)
 
-    multiply(first % 8, first // 8)
-    e_late(0)
+    prepare(first % 8, first // 8)
+    multiply(first % 8, first // 8, (0, 1))
     z_part(0, 0, 0)
     z_part(0, 1, 1)
-    multiply(second % 8, second // 8)
+    multiply(first % 8, first // 8, (1, 2))
+    e_late(0)
+    prepare(second % 8, second // 8)
+    multiply(second % 8, second // 8, (0, 1))
     z_part(1, 0, 1)
-    multiply(third % 8, third // 8)
     z_part(1, 1, 0)
+    multiply(second % 8, second // 8, (1, 2))
     for p in range(1, 8):
         e_late(p)
     z_part(1, 0, 0)
     z_part(1, 1, 1)
     x_step(0)
-    for s in (2, 3):
-        for l in range(2):
-            for way in (0, 1):
-                z_part(s, way, l)
-        x_step(s - 1)
+    for l in (0, 1):
+        for way in (0, 1):
+            z_part(2, way, l)
+    x_step(1)
+    for way in (0, 1):
+        z_part(3, way, 1 - xl)
+    x_step(2)
+    for way in (0, 1):
+        z_part(3, way, xl)
     x_step(3)
 
     for way in (0, 1):
@@ -338,7 +371,7 @@
 
     def write(b):
         for side in range(2):
-            first = (side * NB + b) * LANES
+            first = (2 * b + side) * LANES
             out_ref[:, first:first + LANES] = part[7, xl, b, side * ROWS:side * ROWS + rows]
 
     for b in range(NZ, NB):
@@ -355,6 +388,11 @@
         def _(p=p):
             for copy in e_copies(p):
                 copy.wait_send()
+    for s in range(4):
+        for way in (0, 1):
+            for l in (0, 1) if s > 0 else (way,):
+                for copy in z_copies(way, s, l):
+                    copy.wait_send()
     for copy in started:
         copy.wait_send()
 

time: 95.2 us -> 90.3 us (0.949)
  Pallas kernels: 93 us -> 88.1 us
    pallas_call x1, Pallas kernels: 93 us -> 88.1 us  [on_device(): pl.pallas_call(kernel, out_shape=jax.ShapeDtypeStruct((rows, width), F32)...]
where the time goes in v3:
time: 90.3 us; the launch traced here: 90.1 us
  Pallas kernels  88.1 us (98%)
  local copies, waits for them, and re-layouts  2.07 us (2%)
    pallas_call x1, Pallas kernels, on_device(): pl.pallas_call(kernel, out_shape=jax.ShapeDtypeStruct((rows, width), F32)...  88.1 us
    unnamed x1, local copies, waits for them, and re-layouts  2.07 us

profile of v3, /device:TPU:1, one launch (start us, length us, event | category | flops | bytes accessed | tf_op | source)
XLA Modules:
  0.0 90.1 jit_solution(7876254789024745730)
XLA Ops:
  0.0 88.1 %shard_map.37 = f32[100,1800]{1,0:T(8,128)} custom-call(bf16[100,1800]{1,0:T(8,128)(2,1)} %a_ref.1, s32[2,2]{1,0:T(2,128)} %cd_ref.1, bf16[1800,1800]{1,0:T(8,128)(2,1)} %b_hbm.1), custom_call_target="tpu_custom_call" | custom-call | tf_op jit(solution)/shard_map/pallas_call | solution.py:405
  88.1 2.1 %copy.5 = f32[100,1800]{1,0:T(8,128)} copy(f32[100,1800]{1,0:T(8,128)} %shard_map.37) | data formatting | bytes 1440000

commit v4 on v3

--- a/solution.py
+++ b/solution.py
@@ -22,7 +22,7 @@
 QUAD = 512
 OWN, Y_M, Y_P, Y_2, R_OWN, R_M, R_P, R_2 = range(8)
 LAST = 8
-EARLY = (OWN, Y_M, Y_P, R_OWN, Y_2)
+EARLY = (OWN, Y_M, Y_P)
 
 
 def kernel(a_ref, cd_ref, b_hbm, out_ref, abuf, ebuf, b_ref, part, tmp, left, zs, zr, zsx, zrx, xs, xr, xsx, xrx,
@@ -289,19 +289,18 @@
     arrive_sibling(R_OWN)
     prepare(R_OWN, places[R_OWN])
     multiply(R_OWN, places[R_OWN])
-    e_emit(places[R_OWN])
     for part_of in (1, 2):
         arrive(R_M, part_of)
     arrive(R_P, 0)
     arrive_sibling(Y_2)
     prepare(Y_2, places[Y_2])
     multiply(Y_2, places[Y_2])
-    e_emit(places[Y_2])
     arrive_sibling(R_M)
     prepare(R_M, places[R_M])
-    multiply(R_M, places[R_M])
+    multiply(R_M, places[R_M], (0, 1))
     for part_of in range(3):
         arrive(R_2, part_of)
+    multiply(R_M, places[R_M], (1, 2))
     arrive_sibling(R_P)
     arrive_sibling(R_2)
     keys = [places[n] * 8 + n for n in (R_P, R_2)]

time: 90.3 us -> 89.1 us (0.987)
  Pallas kernels: 88.1 us -> 86.9 us
    pallas_call x1, Pallas kernels: 88.1 us -> 86.9 us  [on_device(): pl.pallas_call(kernel, out_shape=jax.ShapeDtypeStruct((rows, width), F32)...]
where the time goes in v4:
time: 89.1 us; the launch traced here: 89 us
  Pallas kernels  86.9 us (98%)
  local copies, waits for them, and re-layouts  2.07 us (2%)
    pallas_call x1, Pallas kernels, on_device(): pl.pallas_call(kernel, out_shape=jax.ShapeDtypeStruct((rows, width), F32)...  86.9 us
    unnamed x1, local copies, waits for them, and re-layouts  2.07 us

profile of v4, /device:TPU:1, one launch (start us, length us, event | category | flops | bytes accessed | tf_op | source)
XLA Modules:
  0.0 89.0 jit_solution(7092565857616405388)
XLA Ops:
  0.0 86.9 %shard_map.37 = f32[100,1800]{1,0:T(8,128)} custom-call(bf16[100,1800]{1,0:T(8,128)(2,1)} %a_ref.1, s32[2,2]{1,0:T(2,128)} %cd_ref.1, bf16[1800,1800]{1,0:T(8,128)(2,1)} %b_hbm.1), custom_call_target="tpu_custom_call" | custom-call | tf_op jit(solution)/shard_map/pallas_call | solution.py:404
  86.9 2.1 %copy.5 = f32[100,1800]{1,0:T(8,128)} copy(f32[100,1800]{1,0:T(8,128)} %shard_map.37) | data formatting | bytes 1440000

commit v5 on v4

--- a/solution.py
+++ b/solution.py
@@ -341,10 +341,12 @@
     z_part(1, 0, 1)
     z_part(1, 1, 0)
     multiply(second % 8, second // 8, (1, 2))
-    for p in range(1, 8):
-        e_late(p)
+    e_late(1)
+    e_late(2)
     z_part(1, 0, 0)
     z_part(1, 1, 1)
+    for p in range(3, 8):
+        e_late(p)
     x_step(0)
     for l in (0, 1):
         for way in (0, 1):

time: 89.1 us -> 89.1 us (level)
  no operation moved by 1% of the time
where the time goes in v5:
time: 89.1 us; the launch traced here: 89 us
  Pallas kernels  86.9 us (98%)
  local copies, waits for them, and re-layouts  2.07 us (2%)
    pallas_call x1, Pallas kernels, on_device(): pl.pallas_call(kernel, out_shape=jax.ShapeDtypeStruct((rows, width), F32)...  86.9 us
    unnamed x1, local copies, waits for them, and re-layouts  2.07 us

profile of v5, /device:TPU:1, one launch (start us, length us, event | category | flops | bytes accessed | tf_op | source)
XLA Modules:
  0.0 89.0 jit_solution(8587024758298808027)
XLA Ops:
  0.0 86.9 %shard_map.37 = f32[100,1800]{1,0:T(8,128)} custom-call(bf16[100,1800]{1,0:T(8,128)(2,1)} %a_ref.1, s32[2,2]{1,0:T(2,128)} %cd_ref.1, bf16[1800,1800]{1,0:T(8,128)(2,1)} %b_hbm.1), custom_call_target="tpu_custom_call" | custom-call | tf_op jit(solution)/shard_map/pallas_call | solution.py:406
  86.9 2.1 %copy.5 = f32[100,1800]{1,0:T(8,128)} copy(f32[100,1800]{1,0:T(8,128)} %shard_map.37) | data formatting | bytes 1440000
